TPU v7x, 128 devices: a whole 4x4x4 slice. The times are simulated.
128 devices in a mesh: row: 8 (over z, y_hi), col: 16 (over x, y_lo, core).
Axes of the slice: x: 4, y: 4 (y_hi: 2, y_lo: 2; y = y_hi * 2 + y_lo), z: 4, core: 2. Of those that a mesh axis runs over, the one named last changes fastest.
Arguments:
- obj: float32 [2, 2048, 4096], P(None, 'row', 'col'), may hold values from -4.2 to 4.2
- probe: float32 [2, 256, 256], replicated, may hold values from -4.2 to 4.2
- amplitudes: bfloat16 [512, 256, 256], P(('row', 'col')), may hold values from 0.049804688 to 4
- positions: int32 [512, 2], replicated, may hold values from 0 to 3840, as said below
Outputs:
- new_object: float32 [2, 2048, 4096], P(None, 'row', 'col')
- new_probe: float32 [2, 256, 256], replicated
Inputs may be any that keep to these rules, and one draw needn't show every extreme that they name: `positions`: entry p is the top-left cell (row, column) of pattern p's window of 256 x 256 cells, which lies inside the object. Pattern p is held by device p // 4 in row-major order of (row, col), and its row offset lies in that device's band of 256 object rows. One device holds at most 2 patterns whose window starts in one tile, and exactly 2 for some tile in every draw; at most 8 windows start in one tile, and in every row of tiles exactly 8 start in one tile.
All inputs are finite; a program needn't handle non-finite values.
Results may differ from a plain program's by a relative error of at most 0.0018.
Values may be sent and summed in bfloat16 or wider, within the bound.
A program may use at most 128 MiB of HBM per device.

v0:
```python
import jax
import jax.numpy as jnp
from jax import lax
from jax.sharding import PartitionSpec as P

ITERS = 2
SEND = 2
amplitude_floor = 0.1
object_regular = 0.5
probe_regular = 1.0
highest = lax.Precision.HIGHEST


def passed_along(value, axis, steps):
    count = lax.axis_size(axis)
    leading, last = (max(0, -steps), min(count, count - steps))
    return lax.ppermute(value, axis, [(source, source + steps) for source in range(leading, last)])


def dft_tables(order):
    counter = jnp.arange(order, dtype=jnp.int32)
    phases = counter[:, None] * counter[None, :] % order
    angles = phases.astype(jnp.float32) * (2.0 * jnp.pi / order)
    norming = 1.0 / jnp.sqrt(jnp.float32(order))
    return (jnp.cos(angles) * norming, -jnp.sin(angles) * norming)


def left_apply(tables, real_part, imag_part):
    first = jnp.einsum("ab,sbc->sac", tables[0], real_part, precision=highest)
    second = jnp.einsum("ab,sbc->sac", tables[1], imag_part, precision=highest)
    third = jnp.einsum("ab,sbc->sac", tables[2], real_part + imag_part, precision=highest)
    return (first - second, third - first - second)


def right_apply(tables, real_part, imag_part):
    first = jnp.einsum("sab,bc->sac", real_part, tables[0], precision=highest)
    second = jnp.einsum("sab,bc->sac", imag_part, tables[1], precision=highest)
    third = jnp.einsum("sab,bc->sac", real_part + imag_part, tables[2], precision=highest)
    return (first - second, third - first - second)


def transform(tables, real_part, imag_part):
    inner_re, inner_im = right_apply(tables, real_part, imag_part)
    return left_apply(tables, inner_re, inner_im)


def extend_tile(current):
    from_right = passed_along(current, "col", -1)
    widened = jnp.concatenate([current, from_right], axis=2)
    from_below = passed_along(widened, "row", -1)
    return jnp.concatenate([widened, from_below], axis=1)


def fold_tile(sums, tile_rows, tile_cols, order):
    from_above = passed_along(sums[:, tile_rows:, :], "row", 1)
    upper = sums[:, :tile_rows, :].at[:, :order, :].add(from_above)
    from_left = passed_along(upper[:, :, tile_cols:], "col", 1)
    return upper[:, :, :tile_cols].at[:, :, :order].add(from_left)


def local(obj, probe, amplitudes, positions):
    col_count = lax.axis_size("col")
    my_row = lax.axis_index("row")
    my_col = lax.axis_index("col")
    device_id = my_row * col_count + my_col
    tile_rows = obj.shape[1]
    tile_cols = obj.shape[2]
    order = probe.shape[1]
    pat_count = amplitudes.shape[0]
    capacity = 2 * pat_count
    slot_count = col_count * SEND
    band_count = col_count * pat_count
    local_index = jnp.arange(pat_count, dtype=jnp.int32)
    my_ids = device_id * pat_count + local_index
    owner_col = positions[my_ids, 1] // tile_cols
    earlier = local_index[None, :] < local_index[:, None]
    same_owner = owner_col[:, None] == owner_col[None, :]
    send_rank = jnp.sum(same_owner & earlier, axis=1)
    send_slot = owner_col * SEND + send_rank
    placing = (jnp.arange(slot_count, dtype=jnp.int32)[:, None] == send_slot[None, :]).astype(
        jnp.bfloat16
    )
    outgoing = jnp.dot(
        placing, amplitudes.reshape(pat_count, order * order), preferred_element_type=jnp.float32
    ).astype(jnp.bfloat16)
    incoming = lax.all_to_all(outgoing, "col", split_axis=0, concat_axis=0, tiled=True)
    band_first = my_row * band_count
    band_pos = lax.dynamic_slice_in_dim(positions, band_first, band_count, 0)
    band_ids = band_first + jnp.arange(band_count, dtype=jnp.int32)
    in_mine = band_pos[:, 1] // tile_cols == my_col
    mine_count = in_mine.astype(jnp.int32)
    band_rank = jnp.cumsum(mine_count) - mine_count
    selection = (band_rank[None, :] == jnp.arange(capacity, dtype=jnp.int32)[:, None]) & in_mine[
        None, :
    ]
    valid = jnp.any(selection, axis=1)
    listed = jnp.sum(jnp.where(selection, band_ids[None, :], 0), axis=1)
    source_dev = listed // pat_count
    source_col = source_dev % col_count
    before = (
        (source_dev[None, :] == source_dev[:, None])
        & (listed[None, :] < listed[:, None])
        & valid[None, :]
    )
    recv_rank = jnp.sum(before, axis=1)
    recv_slot = source_col * SEND + recv_rank
    picking = (
        (jnp.arange(slot_count, dtype=jnp.int32)[None, :] == recv_slot[:, None]) & valid[:, None]
    ).astype(jnp.bfloat16)
    measured = jnp.dot(picking, incoming, preferred_element_type=jnp.float32).reshape(
        capacity, order, order
    )
    spots = positions[listed]
    offset_y = jnp.where(valid, spots[:, 0] - my_row * tile_rows, 0)
    offset_x = jnp.where(valid, spots[:, 1] - my_col * tile_cols, 0)
    weight = valid.astype(jnp.float32)[:, None, None]
    cos_part, sin_part = dft_tables(order)
    forward = (cos_part, sin_part, cos_part + sin_part)
    inverse = (cos_part, -sin_part, cos_part - sin_part)
    current = obj
    probe_now = probe
    for sweep in range(ITERS):
        extended = extend_tile(current)

        def cut_window(top, left):
            return lax.dynamic_slice(extended, (0, top, left), (2, order, order))

        windows = jax.vmap(cut_window)(offset_y, offset_x)
        win_re = windows[:, 0]
        win_im = windows[:, 1]
        probe_re = probe_now[0]
        probe_im = probe_now[1]
        exit_re = probe_re * win_re - probe_im * win_im
        exit_im = probe_re * win_im + probe_im * win_re
        far_re, far_im = transform(forward, exit_re, exit_im)
        factor = measured / jnp.sqrt(far_re * far_re + far_im * far_im + amplitude_floor)
        back_re, back_im = transform(inverse, far_re * factor, far_im * factor)
        change_re = (back_re - exit_re) * weight
        change_im = (back_im - exit_im) * weight
        power = probe_re * probe_re + probe_im * probe_im
        deposits = jnp.stack(
            [
                probe_re * change_re + probe_im * change_im,
                probe_re * change_im - probe_im * change_re,
                power[None] * weight + 0.0 * change_re,
            ],
            axis=1,
        )

        def deposit(index, total):
            start = (0, offset_y[index], offset_x[index])
            block = lax.dynamic_slice(total, start, (3, order, order))
            return lax.dynamic_update_slice(total, block + deposits[index], start)

        sums = lax.fori_loop(
            0, capacity, deposit, jnp.zeros((3, tile_rows + order, tile_cols + order), jnp.float32)
        )
        partials = jnp.stack(
            [
                jnp.sum(win_re * change_re + win_im * change_im, axis=0),
                jnp.sum(win_re * change_im - win_im * change_re, axis=0),
                jnp.sum((win_re * win_re + win_im * win_im) * weight, axis=0),
            ]
        )
        tile_sums = fold_tile(sums, tile_rows, tile_cols, order)
        current = current + tile_sums[:2] / (tile_sums[2] + object_regular)[None]
        totals = lax.psum(partials, ("row", "col"))
        probe_now = probe_now + totals[:2] / (totals[2] + probe_regular)[None]
    return (current, probe_now)


def solution(mesh):
    placed = (P(None, "row", "col"), P(), P(("row", "col"), None, None), P())
    return jax.shard_map(
        local, mesh=mesh, in_specs=placed, out_specs=(P(None, "row", "col"), P()), check_vma=False
    )
```

profile of v0, /device:TPU:1, one launch (start us, length us, event | category | flops | bytes accessed | tf_op | source)
XLA Modules:
  0.0 974.0 jit_solution(13523694036995378047)
XLA Ops:
  7.2 3.3 collective-permute-start
  13.5 3.2 convolution_convert_fusion
  16.7 5.9 all_to_all.8
  22.6 5.7 all-to-all-start
  34.0 65.7 %collective-permute-done.1 = f32[2,256,512]{2,1,0:T(8,128)} collective-permute-done((f32[2,256,512]{2,1,0:T(8,128)S(1)}, f32[2,256,512]{2,1,0:T(8,128)}, u32[]{:S(2)}, u32[]{:S(2)}) %collective-permute-start.1) | collective-permute-done | bytes 1048608 | tf_op jit(solution)/shard_map/ppermute | solution.py:17
  103.5 25.5 %while.38 = (s32[]{:T(128)}, f32[2,512,512]{2,1,0:T(8,128)S(1)}, s32[8,3]{0,1:T(4,128)S(1)}, f32[8,2,256,256]{2,3,0,1:T(8,128)}, s32[]{:T(128)}) while((s32[]{:T(128)}, f32[2,512,512]{2,1,0:T(8,128)S(1)}, s32[8,3]{0,1:T(4,128)S(1)}, f32[8,2,256,256]{2,3,0,1:T(8,128)}, s32[]{:T(128)}) %tuple.156), condition=%wide.while_cond.4, body=%wide.while_body.4.sunk | while | flops 2 | bytes 3145853 | solution.py:126
  131.8 4.4 fusion.114
  136.2 4.4 fusion.126
  140.7 5.0 subtract_subtract_fusion.3
  145.7 5.6 fusion.112
  151.3 5.7 fusion.79
  157.0 5.5 all_to_all.10
  162.4 4.3 fusion
  166.7 2.9 copy.167
  169.6 12.4 %fusion.48 = (f32[8,256,256]{1,2,0:T(8,128)S(1)}, f32[8,256,256]{1,2,0:T(8,128)S(1)}) fusion(f32[8,256,256]{1,2,0:T(8,128)} %copy.167, f32[8,256,256]{2,1,0:T(8,128)} %fusion.112, f32[8,256,256]{2,1,0:T(8,128)} %fusion.79, f32[8,256,256]{2,1,0:T(8,128)} %copy-done.9, f32[8,256,256]{2,1,0:T(8,128)} %copy-done.4, f32[8,256,256]{2,1,0:T(8,128)} %copy-done.3), kind=kOutput, calls=%fused_computation.104 | convolution fusion | flops 1618083840 | bytes 16777216 | tf_op jit(solution)/shard_map/ab,sbc->sac/dot_general | solution.py:31
  182.0 4.5 fusion.102
  186.5 4.5 fusion.123
  190.9 4.9 subtract_subtract_fusion.2
  195.8 4.5 fusion.76
  200.3 4.4 fusion.100
  204.8 6.5 fusion.27
  212.1 3.3 pad_maximum_fusion
  217.5 134.4 %while.36 = (s32[]{:T(128)}, f32[3,512,512]{2,1,0:T(8,128)}, s32[8]{0:T(128)S(1)}, s32[8]{0:T(128)S(1)}, f32[8,3,256,256]{2,3,0,1:T(8,128)}, /*index=5*/s32[]{:T(128)}, s32[]{:T(128)}, s32[]{:T(128)}) while((s32[]{:T(128)}, f32[3,512,512]{2,1,0:T(8,128)}, s32[8]{0:T(128)S(1)}, s32[8]{0:T(128)S(1)}, f32[8,3,256,256]{2,3,0,1:T(8,128)}, ...), condition=%wide.region_6.7_spmd, body=%wide.region_5.6_spmd.sunk | while | flops 196616 | bytes 7078089 | solution.py:155
  225.6 8.9 dynamic_update_slice.16
  242.7 8.9 dynamic_update_slice.16
  259.7 9.4 dynamic_update_slice.16
  277.2 9.0 dynamic_update_slice.16
  294.3 8.3 dynamic_update_slice.16
  310.7 8.3 dynamic_update_slice.16
  327.2 8.3 dynamic_update_slice.16
  343.6 8.3 dynamic_update_slice.16
  353.7 3.8 collective-permute-start.2
  357.5 31.8 %collective-permute-done.2 = f32[3,256,512]{2,1,0:T(8,128)S(1)} collective-permute-done((f32[3,256,512]{2,1,0:T(8,128)S(1)}, f32[3,256,512]{2,1,0:T(8,128)S(1)}, u32[]{:S(2)}, u32[]{:S(2)}) %collective-permute-start.2) | collective-permute-done | bytes 1572896 | tf_op jit(solution)/shard_map/ppermute | solution.py:17
  389.7 6.2 collective-permute-start.3
  396.0 8.9 collective-permute-done.3
  408.2 8.3 collective-permute-done.4
  418.1 147.8 %all-reduce.4.cloned.1.call-done = f32[3,256,256]{1,2,0:T(8,128)} async-done(((f32[3,256,256]{1,2,0:T(8,128)}), f32[3,256,256]{1,2,0:T(8,128)}) %all-reduce.4.cloned.1.call-update) | async-done | bytes 786448 | tf_op jit(solution)/shard_map/psum | solution.py:167
  572.9 25.8 %while.39 = (s32[]{:T(128)}, f32[2,512,512]{2,1,0:T(8,128)S(1)}, s32[8,3]{0,1:T(4,128)S(1)}, f32[8,2,256,256]{2,3,0,1:T(8,128)}, s32[]{:T(128)}) while((s32[]{:T(128)}, f32[2,512,512]{2,1,0:T(8,128)S(1)}, s32[8,3]{0,1:T(4,128)S(1)}, f32[8,2,256,256]{2,3,0,1:T(8,128)}, s32[]{:T(128)}) %tuple.172), condition=%wide.while_cond.5, body=%wide.while_body.5.sunk | while | flops 2 | bytes 3145853 | solution.py:126
  601.5 4.5 fusion.110
  606.0 4.5 fusion.120
  610.5 4.9 subtract_subtract_fusion.1
  615.4 4.5 fusion.73
  619.9 4.4 fusion.108
  624.3 5.5 fusion.38
  629.9 4.5 fusion.98
  634.4 4.6 fusion.117
  639.0 4.6 subtract_subtract_fusion
  643.6 4.5 fusion.70
  648.2 4.7 fusion.96
  652.9 6.9 fusion.12
  660.6 3.3 pad_maximum_fusion.1
  666.0 133.6 %while.37 = (s32[]{:T(128)}, f32[3,512,512]{2,1,0:T(8,128)}, s32[8]{0:T(128)S(1)}, s32[8]{0:T(128)S(1)}, f32[8,3,256,256]{2,3,0,1:T(8,128)}, /*index=5*/s32[]{:T(128)}, s32[]{:T(128)}, s32[]{:T(128)}) while((s32[]{:T(128)}, f32[3,512,512]{2,1,0:T(8,128)}, s32[8]{0:T(128)S(1)}, s32[8]{0:T(128)S(1)}, f32[8,3,256,256]{2,3,0,1:T(8,128)}, ...), condition=%wide.region_12.13_spmd, body=%wide.region_11.12_spmd.sunk | while | flops 196616 | bytes 7078089 | solution.py:155
  674.0 8.9 dynamic_update_slice.17
  690.9 8.9 dynamic_update_slice.17
  707.9 9.4 dynamic_update_slice.17
  725.3 9.0 dynamic_update_slice.17
  742.3 8.3 dynamic_update_slice.17
  758.6 8.3 dynamic_update_slice.17
  775.0 8.3 dynamic_update_slice.17
  791.3 8.3 dynamic_update_slice.17
  802.5 5.0 collective-permute-start.6
  808.5 30.1 %collective-permute-done.6 = f32[3,256,512]{2,1,0:T(8,128)} collective-permute-done((f32[3,256,512]{2,1,0:T(8,128)}, f32[3,256,512]{2,1,0:T(8,128)}, u32[]{:S(2)}, u32[]{:S(2)}) %collective-permute-start.6) | collective-permute-done | bytes 1572896 | tf_op jit(solution)/shard_map/ppermute | solution.py:17
  841.6 5.9 collective-permute-start.7
  847.6 114.0 %all-reduce.6.cloned.1.call-done = f32[3,256,256]{1,2,0:T(8,128)} async-done(((f32[3,256,256]{1,2,0:T(8,128)}), f32[3,256,256]{1,2,0:T(8,128)}) %all-reduce.6.cloned.1.call-update) | async-done | bytes 786448 | tf_op jit(solution)/shard_map/psum | solution.py:167
  (298 shorter events, 168.2 us)
Async XLA Ops:
  7.2 23.1 %collective-permute-start = (f32[2,256,256]{2,1,0:T(8,128)}, f32[2,256,256]{2,1,0:T(8,128)S(1)}, u32[]{:S(2)}, u32[]{:S(2)}) collective-permute-start(f32[2,256,256]{2,1,0:T(8,128)} %param.24), channel_id=1, source_target_pairs={{1,0},{2,1},{3,2},{4,3},{5,4},{6,5},{7,6},{8,7},{9,8},{10,9},{11,1... | collective-permute-start | bytes 1572872 | tf_op jit(solution)/shard_map/ppermute | solution.py:17
  22.6 5.7 copy-start
  22.6 7.4 copy-start.19
  22.6 134.4 %all-to-all-start = ((bf16[16,2,65536]{2,1,0:T(2,128)(2,1)}), bf16[16,2,65536]{2,1,0:T(2,128)(2,1)}, u32[]{:S(2)}, u32[]{:S(2)}) async-start(bf16[16,2,65536]{2,1,0:T(2,128)(2,1)} %all_to_all.8), calls=%async_computation | async-start | bytes 8388608 | tf_op jit(solution)/shard_map/all_to_all | solution.py:86
  28.3 3.6 copy-start.21
  28.3 537.6 %all-reduce.4.cloned.1.call-start = ((), (), s32[]{:S(2)}) async-start(), calls=%async_computation.1 | async-start | bytes 1572864 | tf_op jit(solution)/shard_map/psum | solution.py:167
  30.4 69.3 %collective-permute-start.1 = (f32[2,256,512]{2,1,0:T(8,128)S(1)}, f32[2,256,512]{2,1,0:T(8,128)}, u32[]{:S(2)}, u32[]{:S(2)}) collective-permute-start(f32[2,256,512]{2,1,0:T(8,128)S(1)} %constant_dynamic-update-slice_fusion.2), channel_id=1, source_target_pairs={{16,0},{32,16},{48,32},{64,48},{80,64},{96,80},{112,96},{17,1},{33... | collective-permute-start | bytes 3145736 | tf_op jit(solution)/shard_map/ppermute | solution.py:17
  131.8 8.9 copy-start.1
  136.2 15.1 %copy-start.3 = (f32[8,256,256]{2,1,0:T(8,128)}, f32[8,256,256]{2,1,0:T(8,128)S(1)}, u32[]{:S(2)}) copy-start(f32[8,256,256]{2,1,0:T(8,128)S(1)} %fusion.114) | copy-start | bytes 6291460
  140.7 10.6 %copy-start.4 = (f32[8,256,256]{2,1,0:T(8,128)}, f32[8,256,256]{2,1,0:T(8,128)S(1)}, u32[]{:S(2)}) copy-start(f32[8,256,256]{2,1,0:T(8,128)S(1)} %fusion.126) | copy-start | bytes 6291460
  145.7 5.6 copy-start.9
  195.8 9.0 copy-start.7
  200.3 4.5 copy-start.2
  204.8 6.5 copy-start.18
  204.8 6.5 copy-start.29
  352.0 37.3 %copy-start.6 = (f32[3,512,512]{2,1,0:T(8,128)S(1)}, f32[3,512,512]{2,1,0:T(8,128)}, u32[]{:S(2)}) copy-start(f32[3,512,512]{2,1,0:T(8,128)} %get-tuple-element.270) | copy-start | bytes 9437188
  353.7 35.6 %collective-permute-start.2 = (f32[3,256,512]{2,1,0:T(8,128)S(1)}, f32[3,256,512]{2,1,0:T(8,128)S(1)}, u32[]{:S(2)}, u32[]{:S(2)}) collective-permute-start(f32[3,256,512]{2,1,0:T(8,128)S(1)} %slice.165), channel_id=1, source_target_pairs={{0,16},{16,32},{32,48},{48,64},{64,80},{80,96},{96,112},{1,17},{17... | collective-permute-start | bytes 4718600 | tf_op jit(solution)/shard_map/ppermute | solution.py:17
  389.6 15.4 %copy-start.20 = (f32[2,256,256]{2,1,0:T(8,128)S(1)}, f32[2,256,256]{2,1,0:T(8,128)}, u32[]{:S(2)}) copy-start(f32[2,256,256]{2,1,0:T(8,128)} %param.24) | copy-start | bytes 1572868
  389.7 15.2 %collective-permute-start.3 = (f32[3,256,256]{2,1,0:T(8,128)S(1)}, f32[3,256,256]{2,1,0:T(8,128)S(1)}, u32[]{:S(2)}, u32[]{:S(2)}) collective-permute-start(f32[3,256,256]{2,1,0:T(8,128)S(1)} %slice.219), channel_id=1, source_target_pairs={{0,1},{1,2},{2,3},{3,4},{4,5},{5,6},{6,7},{7,8},{8,9},{9,10},{10,1... | collective-permute-start | bytes 2359304 | tf_op jit(solution)/shard_map/ppermute | solution.py:17
  405.2 163.9 %copy-start.11 = (f32[2,256,256]{2,1,0:T(8,128)}, f32[2,256,256]{2,1,0:T(8,128)S(1)}, u32[]{:S(2)}) copy-start(f32[2,256,256]{2,1,0:T(8,128)S(1)} %fusion.84) | copy-start | bytes 1572868
  405.2 11.2 %collective-permute-start.4 = (f32[2,256,256]{2,1,0:T(8,128)S(1)}, f32[2,256,256]{2,1,0:T(8,128)S(1)}, u32[]{:S(2)}, u32[]{:S(2)}) collective-permute-start(f32[2,256,256]{2,1,0:T(8,128)S(1)} %fusion.84), channel_id=1, source_target_pairs={{1,0},{2,1},{3,2},{4,3},{5,4},{6,5},{7,6},{8,7},{9,8},{10,9},{11,1... | collective-permute-start | bytes 1572872 | tf_op jit(solution)/shard_map/ppermute | solution.py:17
  407.1 10.8 %copy-start.22 = (f32[2,256,256]{2,1,0:T(8,128)S(1)}, f32[2,256,256]{2,1,0:T(8,128)}, u32[]{:S(2)}) copy-start(f32[2,256,256]{2,1,0:T(8,128)} %param.25) | copy-start | bytes 1572868
  408.1 553.5 %all-reduce.6.cloned.1.call-start = ((), (), s32[]{:S(2)}) async-start(), calls=%async_computation.2 | async-start | bytes 1572864 | tf_op jit(solution)/shard_map/psum | solution.py:167
  416.4 1.4 copy-start.23
  416.6 152.5 %collective-permute-start.5 = (f32[2,256,512]{2,1,0:T(8,128)S(1)}, f32[2,256,512]{2,1,0:T(8,128)}, u32[]{:S(2)}, u32[]{:S(2)}) collective-permute-start(f32[2,256,512]{2,1,0:T(8,128)S(1)} %pad_maximum_fusion.4), channel_id=1, source_target_pairs={{16,0},{32,16},{48,32},{64,48},{80,64},{96,80},{112,96},{17,1},{33... | collective-permute-start | bytes 3145736 | tf_op jit(solution)/shard_map/ppermute | solution.py:17
  565.9 3.2 copy-start.24
  568.1 1.0 copy-start.15
  619.9 4.5 copy-start.10
  648.1 4.7 copy-start.8
  652.8 6.9 copy-start.17
  652.8 6.9 copy-start.28
  799.7 7.9 copy-start.25
  799.7 7.9 copy-start.26
  799.7 7.9 copy-start.27
  799.7 38.9 %copy-start.5 = (f32[3,512,512]{2,1,0:T(8,128)S(1)}, f32[3,512,512]{2,1,0:T(8,128)}, u32[]{:S(2)}) copy-start(f32[3,512,512]{2,1,0:T(8,128)} %get-tuple-element.271) | copy-start | bytes 9437188
  802.5 36.1 %collective-permute-start.6 = (f32[3,256,512]{2,1,0:T(8,128)}, f32[3,256,512]{2,1,0:T(8,128)}, u32[]{:S(2)}, u32[]{:S(2)}) collective-permute-start(f32[3,256,512]{2,1,0:T(8,128)} %slice.177), channel_id=1, source_target_pairs={{0,16},{16,32},{32,48},{48,64},{64,80},{80,96},{96,112},{1,17},{17... | collective-permute-start | bytes 4718600 | tf_op jit(solution)/shard_map/ppermute | solution.py:17
  840.4 1.2 copy-start.13
  841.5 121.0 %copy-start.16 = (f32[2,256,256]{1,2,0:T(8,128)S(1)}, f32[2,256,256]{1,2,0:T(8,128)}, u32[]{:S(2)}) copy-start(f32[2,256,256]{1,2,0:T(8,128)} %copy-done.15) | copy-start | bytes 1572868
  841.6 123.1 %copy-start.14 = (f32[3,256,512]{2,1,0:T(8,128)S(1)}, f32[3,256,512]{2,1,0:T(8,128)}, u32[]{:S(2)}) copy-start(f32[3,256,512]{2,1,0:T(8,128)} %copy-done.13) | copy-start | bytes 4718596
  841.6 123.1 %collective-permute-start.7 = (f32[3,256,256]{2,1,0:T(8,128)S(1)}, f32[3,256,256]{2,1,0:T(8,128)}, u32[]{:S(2)}, u32[]{:S(2)}) collective-permute-start(f32[3,256,256]{2,1,0:T(8,128)S(1)} %slice.227), channel_id=1, source_target_pairs={{0,1},{1,2},{2,3},{3,4},{4,5},{5,6},{6,7},{7,8},{8,9},{9,10},{10,1... | collective-permute-start | bytes 2359304 | tf_op jit(solution)/shard_map/ppermute | solution.py:17
  963.7 2.3 copy-start.12
Sparse Core Ops, SparseCore 0:
  408.2 157.6 all-reduce.3
  808.6 152.9 all-reduce.5
where the time goes:
time: 985 us; the launch traced here: 974 us
  waiting for transfers between devices  407 us (41%)
  local copies, waits for them, and re-layouts  268 us (27%)
  matrix products  132 us (13%)
  loops' own time  61.9 us (6%)
  other arithmetic  55.1 us (6%)
  starting transfers between devices  34.6 us (4%)
  between operations  15.1 us (2%)
    psum x2, waiting for transfers between devices, local(): totals = lax.psum(partials, ('row', 'col'))  262 us
    ppermute x8, waiting for transfers between devices, passed_along(): lax.ppermute(value, axis, [(source, source + steps) for source in range(l...  145 us
    dynamic_update_slice x16, local copies, waits for them, and re-layouts, deposit(): return lax.dynamic_update_slice(total, block + deposits[index], start)  139 us
    another operation x2, loops' own time, local(): lax.fori_loop(0, capacity, deposit, jnp.zeros((3, tile_rows + order, tile...  61.4 us
    gather x80, local copies, waits for them, and re-layouts  50.8 us
    dot_general x4, matrix products, left_apply(): jnp.einsum('ab,sbc->sac', tables[2], real_part + imag_part, precision=hig...  31.3 us
    ppermute x8, starting transfers between devices, passed_along(): lax.ppermute(value, axis, [(source, source + steps) for source in range(l...  28.9 us
    add x16, other arithmetic, deposit(): return lax.dynamic_update_slice(total, block + deposits[index], start)  25.4 us
  transfers between devices with their start and end apart: 11, of which 7 were waited for; matrix products, arithmetic and copies ran while one was open for 8% of the time, Pallas kernels for 0%

commit v1 on v0

--- a/solution.py
+++ b/solution.py
@@ -164,7 +164,7 @@
         )
         tile_sums = fold_tile(sums, tile_rows, tile_cols, order)
         current = current + tile_sums[:2] / (tile_sums[2] + object_regular)[None]
-        totals = lax.psum(partials, ("row", "col"))
+        totals = jnp.sum(lax.all_gather(partials, ("row", "col")), axis=0)
         probe_now = probe_now + totals[:2] / (totals[2] + probe_regular)[None]
     return (current, probe_now)
 

time: 985 us -> 1560 us (1.58)
  waiting for transfers between devices: 407 us -> 889 us
  other arithmetic: 55.1 us -> 113 us
  starting transfers between devices: 34.6 us -> 56.2 us
    all_gather x0 -> x2, waiting for transfers between devices: none -> 642 us  [local(): totals = jnp.sum(lax.all_gather(partials, ('row', 'col')), axis=0)]
    psum x2 -> x0, waiting for transfers between devices: 262 us -> none  [local(): totals = lax.psum(partials, ('row', 'col'))]
    ppermute x8, waiting for transfers between devices: 145 us -> 247 us  [passed_along(): lax.ppermute(value, axis, [(source, source + steps) for source in range(l...]
    reduce_sum x0 -> x2, other arithmetic: none -> 61.4 us  [local(): totals = jnp.sum(lax.all_gather(partials, ('row', 'col')), axis=0)]
    ppermute x8, starting transfers between devices: 28.9 us -> 50.4 us  [passed_along(): lax.ppermute(value, axis, [(source, source + steps) for source in range(l...]
  transfers between devices with their start and end apart: 11 -> 11, of which waited for: 7 -> 9; matrix products, arithmetic and copies ran while one was open for 8% -> 21% of each run, Pallas kernels for 0% -> 0%
where the time goes in v1:
time: 1560 us; the launch traced here: 1540 us
  waiting for transfers between devices  889 us (57%)
  local copies, waits for them, and re-layouts  270 us (17%)
  matrix products  135 us (9%)
  other arithmetic  113 us (7%)
  loops' own time  62.9 us (4%)
  starting transfers between devices  56.2 us (4%)
    all_gather x2, waiting for transfers between devices, local(): totals = jnp.sum(lax.all_gather(partials, ('row', 'col')), axis=0)  642 us
    ppermute x8, waiting for transfers between devices, passed_along(): lax.ppermute(value, axis, [(source, source + steps) for source in range(l...  247 us
    dynamic_update_slice x16, local copies, waits for them, and re-layouts, deposit(): return lax.dynamic_update_slice(total, block + deposits[index], start)  139 us
    another operation x2, loops' own time, local(): lax.fori_loop(0, capacity, deposit, jnp.zeros((3, tile_rows + order, tile...  62.6 us
    reduce_sum x2, other arithmetic, local(): totals = jnp.sum(lax.all_gather(partials, ('row', 'col')), axis=0)  61.4 us
    gather x80, local copies, waits for them, and re-layouts  51.6 us
    ppermute x8, starting transfers between devices, passed_along(): lax.ppermute(value, axis, [(source, source + steps) for source in range(l...  50.4 us
    dot_general x4, matrix products, left_apply(): jnp.einsum('ab,sbc->sac', tables[2], real_part + imag_part, precision=hig...  33.8 us
  transfers between devices with their start and end apart: 11, of which 9 were waited for; matrix products, arithmetic and copies ran while one was open for 21% of the time, Pallas kernels for 0%

profile of v1, /device:TPU:1, one launch (start us, length us, event | category | flops | bytes accessed | tf_op | source)
XLA Modules:
  0.0 1541.1 jit_solution(6823508255095513549)
XLA Ops:
  7.2 3.3 collective-permute-start
  16.7 5.9 all_to_all.8
  22.6 5.7 all-to-all-start
  33.8 65.9 %collective-permute-done.1 = f32[2,256,512]{2,1,0:T(8,128)} collective-permute-done((f32[2,256,512]{2,1,0:T(8,128)S(1)}, f32[2,256,512]{2,1,0:T(8,128)}, u32[]{:S(2)}, u32[]{:S(2)}) %collective-permute-start.1) | collective-permute-done | bytes 1048608 | tf_op jit(solution)/shard_map/ppermute | solution.py:17
  103.4 26.0 %while.38 = (s32[]{:T(128)}, f32[2,512,512]{2,1,0:T(8,128)S(1)}, s32[8,3]{0,1:T(4,128)S(1)}, f32[8,2,256,256]{2,3,0,1:T(8,128)}, s32[]{:T(128)}) while((s32[]{:T(128)}, f32[2,512,512]{2,1,0:T(8,128)S(1)}, s32[8,3]{0,1:T(4,128)S(1)}, f32[8,2,256,256]{2,3,0,1:T(8,128)}, s32[]{:T(128)}) %tuple.154), condition=%wide.while_cond.4, body=%wide.while_body.4.sunk | while | flops 2 | bytes 3146353 | solution.py:126
  132.3 4.4 fusion.114
  136.7 4.4 fusion.126
  141.2 5.0 subtract_subtract_fusion.3
  146.2 5.6 fusion.112
  151.8 5.7 fusion.79
  157.5 5.4 all_to_all.10
  162.9 4.3 fusion
  170.1 12.4 fusion.48
  182.5 4.4 fusion.102
  186.9 4.5 fusion.123
  191.4 4.7 fusion.76
  196.1 4.6 subtract_subtract_fusion.2
  200.8 4.4 fusion.100
  205.2 8.4 fusion.27
  224.0 135.1 %while.36 = (s32[]{:T(128)}, f32[3,512,512]{2,1,0:T(8,128)}, s32[8]{0:T(128)S(1)}, s32[8]{0:T(128)S(1)}, f32[8,3,256,256]{2,3,0,1:T(8,128)}, /*index=5*/s32[]{:T(128)}, s32[]{:T(128)}, s32[]{:T(128)}) while((s32[]{:T(128)}, f32[3,512,512]{2,1,0:T(8,128)}, s32[8]{0:T(128)S(1)}, s32[8]{0:T(128)S(1)}, f32[8,3,256,256]{2,3,0,1:T(8,128)}, ...), condition=%wide.region_6.7_spmd, body=%wide.region_5.6_spmd.sunk | while | flops 196616 | bytes 7078081 | solution.py:155
  232.1 8.9 dynamic_update_slice.16
  249.2 8.9 dynamic_update_slice.16
  266.2 9.4 dynamic_update_slice.16
  283.9 9.0 dynamic_update_slice.16
  301.1 8.4 dynamic_update_slice.16
  317.6 8.4 dynamic_update_slice.16
  334.2 8.4 dynamic_update_slice.16
  350.7 8.4 dynamic_update_slice.16
  360.8 3.8 collective-permute-start.2
  364.6 31.8 %collective-permute-done.2 = f32[3,256,512]{2,1,0:T(8,128)S(1)} collective-permute-done((f32[3,256,512]{2,1,0:T(8,128)S(1)}, f32[3,256,512]{2,1,0:T(8,128)S(1)}, u32[]{:S(2)}, u32[]{:S(2)}) %collective-permute-start.2) | collective-permute-done | bytes 1572896 | tf_op jit(solution)/shard_map/ppermute | solution.py:17
  396.8 6.4 collective-permute-start.3
  403.2 8.9 collective-permute-done.3
  414.3 9.7 collective-permute-done.4
  425.5 90.8 %collective-permute-done.5 = f32[2,256,512]{2,1,0:T(8,128)} collective-permute-done((f32[2,256,512]{2,1,0:T(8,128)S(1)}, f32[2,256,512]{2,1,0:T(8,128)}, u32[]{:S(2)}, u32[]{:S(2)}) %collective-permute-start.5) | collective-permute-done | bytes 1048608 | tf_op jit(solution)/shard_map/ppermute | solution.py:17
  520.2 25.9 %while.39 = (s32[]{:T(128)}, f32[2,512,512]{2,1,0:T(8,128)S(1)}, s32[8,3]{0,1:T(4,128)S(1)}, f32[8,2,256,256]{2,3,0,1:T(8,128)}, s32[]{:T(128)}) while((s32[]{:T(128)}, f32[2,512,512]{2,1,0:T(8,128)S(1)}, s32[8,3]{0,1:T(4,128)S(1)}, f32[8,2,256,256]{2,3,0,1:T(8,128)}, s32[]{:T(128)}) %tuple.170), condition=%wide.while_cond.5, body=%wide.while_body.5.sunk | while | flops 2 | bytes 3146353 | solution.py:126
  546.0 263.6 %all-gather.5.cloned.1.call-done = f32[384,256,256]{2,1,0:T(8,128)} async-done(((f32[3,256,256]{2,1,0:T(8,128)}), f32[384,256,256]{2,1,0:T(8,128)}) %all-gather.5.cloned.1.call-update) | async-done | bytes 100663312 | tf_op jit(solution)/shard_map/all_gather | solution.py:167
  809.6 30.8 %reduce_sum.108 = f32[3,256,256]{2,1,0:T(8,128)S(1)} reduce(f32[128,3,256,256]{3,2,1,0:T(8,128)} %bitcast.35, f32[]{:T(128)} %constant.268.clone.1), dimensions={0}, to_apply=%region_10.11 | reduce | flops 24969216 | bytes 101449728 | tf_op jit(solution)/shard_map/reduce_sum | solution.py:167
  844.5 4.5 fusion.110
  849.0 4.4 fusion.120
  853.4 4.7 fusion.73
  858.1 4.7 subtract_subtract_fusion.1
  862.8 4.4 fusion.108
  867.3 5.5 fusion.38
  872.8 4.4 fusion.117
  877.3 4.6 fusion.98
  881.9 4.5 fusion.70
  886.4 4.6 subtract_subtract_fusion
  891.1 4.7 fusion.96
  895.8 7.4 fusion.12
  913.5 134.9 %while.37 = (s32[]{:T(128)}, f32[3,512,512]{2,1,0:T(8,128)}, s32[8]{0:T(128)S(1)}, s32[8]{0:T(128)S(1)}, f32[8,3,256,256]{2,3,0,1:T(8,128)}, /*index=5*/s32[]{:T(128)}, s32[]{:T(128)}, s32[]{:T(128)}) while((s32[]{:T(128)}, f32[3,512,512]{2,1,0:T(8,128)}, s32[8]{0:T(128)S(1)}, s32[8]{0:T(128)S(1)}, f32[8,3,256,256]{2,3,0,1:T(8,128)}, ...), condition=%wide.region_12.13_spmd, body=%wide.region_11.12_spmd.sunk | while | flops 196616 | bytes 7078081 | solution.py:155
  921.6 8.9 dynamic_update_slice.17
  938.6 8.9 dynamic_update_slice.17
  955.7 9.4 dynamic_update_slice.17
  973.2 9.0 dynamic_update_slice.17
  990.4 8.4 dynamic_update_slice.17
  1006.9 8.4 dynamic_update_slice.17
  1023.5 8.4 dynamic_update_slice.17
  1040.0 8.4 dynamic_update_slice.17
  1050.2 21.7 %collective-permute-start.6 = (f32[3,256,512]{2,1,0:T(8,128)S(1)}, f32[3,256,512]{2,1,0:T(8,128)S(1)}, u32[]{:S(2)}, u32[]{:S(2)}) collective-permute-start(f32[3,256,512]{2,1,0:T(8,128)S(1)} %slice.177), channel_id=1, source_target_pairs={{0,16},{16,32},{32,48},{48,64},{64,80},{80,96},{96,112},{1,17},{17... | collective-permute-start | bytes 4718600 | tf_op jit(solution)/shard_map/ppermute | solution.py:17
  1071.9 31.1 %collective-permute-done.6 = f32[3,256,512]{2,1,0:T(8,128)S(1)} collective-permute-done((f32[3,256,512]{2,1,0:T(8,128)S(1)}, f32[3,256,512]{2,1,0:T(8,128)S(1)}, u32[]{:S(2)}, u32[]{:S(2)}) %collective-permute-start.6) | collective-permute-done | bytes 1572896 | tf_op jit(solution)/shard_map/ppermute | solution.py:17
  1103.4 10.7 collective-permute-start.7
  1114.1 8.9 collective-permute-done.7
  1124.1 378.5 %all-gather.7.cloned.1.call-done = f32[384,256,256]{2,1,0:T(8,128)} async-done(((f32[3,256,256]{2,1,0:T(8,128)}), f32[384,256,256]{2,1,0:T(8,128)}) %all-gather.7.cloned.1.call-update) | async-done | bytes 100663312 | tf_op jit(solution)/shard_map/all_gather | solution.py:167
  1502.5 30.6 %reduce_sum.112 = f32[3,256,256]{2,1,0:T(8,128)S(1)} reduce(f32[128,3,256,256]{3,2,1,0:T(8,128)} %bitcast.55, f32[]{:T(128)} %constant.268.clone.1), dimensions={0}, to_apply=%region_16.17 | reduce | flops 24969216 | bytes 101449728 | tf_op jit(solution)/shard_map/reduce_sum | solution.py:167
  (285 shorter events, 178.8 us)
Async XLA Ops:
  7.2 22.9 %collective-permute-start = (f32[2,256,256]{2,1,0:T(8,128)}, f32[2,256,256]{2,1,0:T(8,128)S(1)}, u32[]{:S(2)}, u32[]{:S(2)}) collective-permute-start(f32[2,256,256]{2,1,0:T(8,128)} %param.24), channel_id=1, source_target_pairs={{1,0},{2,1},{3,2},{4,3},{5,4},{6,5},{7,6},{8,7},{9,8},{10,9},{11,1... | collective-permute-start | bytes 1572872 | tf_op jit(solution)/shard_map/ppermute | solution.py:17
  22.6 5.7 copy-start
  22.6 7.4 copy-start.17
  22.6 134.9 %all-to-all-start = ((bf16[16,2,65536]{2,1,0:T(2,128)(2,1)}), bf16[16,2,65536]{2,1,0:T(2,128)(2,1)}, u32[]{:S(2)}, u32[]{:S(2)}) async-start(bf16[16,2,65536]{2,1,0:T(2,128)(2,1)} %all_to_all.8), calls=%async_computation | async-start | bytes 8388608 | tf_op jit(solution)/shard_map/all_to_all | solution.py:86
  28.2 3.6 copy-start.19
  28.2 781.4 %all-gather.5.cloned.1.call-start = ((), (), s32[]{:S(2)}) async-start(), calls=%async_computation.1 | async-start | bytes 101449728 | tf_op jit(solution)/shard_map/all_gather | solution.py:167
  30.2 69.5 %collective-permute-start.1 = (f32[2,256,512]{2,1,0:T(8,128)S(1)}, f32[2,256,512]{2,1,0:T(8,128)}, u32[]{:S(2)}, u32[]{:S(2)}) collective-permute-start(f32[2,256,512]{2,1,0:T(8,128)S(1)} %constant_dynamic-update-slice_fusion.2), channel_id=1, source_target_pairs={{16,0},{32,16},{48,32},{64,48},{80,64},{96,80},{112,96},{17,1},{33... | collective-permute-start | bytes 3145736 | tf_op jit(solution)/shard_map/ppermute | solution.py:17
  132.3 8.9 copy-start.1
  136.7 15.1 copy-start.3
  141.2 10.6 copy-start.4
  146.2 5.6 copy-start.9
  196.1 9.1 copy-start.7
  200.7 4.5 copy-start.2
  213.7 2.4 copy-start.11
  213.7 2.4 copy-start.14
  215.0 1287.6 %all-gather.7.cloned.1.call-start = ((), (), s32[]{:S(2)}) async-start(), calls=%async_computation.2 | async-start | bytes 101449728 | tf_op jit(solution)/shard_map/all_gather | solution.py:167
  359.1 37.3 %copy-start.5 = (f32[3,512,512]{2,1,0:T(8,128)S(1)}, f32[3,512,512]{2,1,0:T(8,128)}, u32[]{:S(2)}) copy-start(f32[3,512,512]{2,1,0:T(8,128)} %get-tuple-element.270) | copy-start | bytes 9437188
  360.8 35.6 %collective-permute-start.2 = (f32[3,256,512]{2,1,0:T(8,128)S(1)}, f32[3,256,512]{2,1,0:T(8,128)S(1)}, u32[]{:S(2)}, u32[]{:S(2)}) collective-permute-start(f32[3,256,512]{2,1,0:T(8,128)S(1)} %slice.165), channel_id=1, source_target_pairs={{0,16},{16,32},{32,48},{48,64},{64,80},{80,96},{96,112},{1,17},{17... | collective-permute-start | bytes 4718600 | tf_op jit(solution)/shard_map/ppermute | solution.py:17
  396.7 15.6 %copy-start.18 = (f32[2,256,256]{2,1,0:T(8,128)S(1)}, f32[2,256,256]{2,1,0:T(8,128)}, u32[]{:S(2)}) copy-start(f32[2,256,256]{2,1,0:T(8,128)} %param.24) | copy-start | bytes 1572868
  396.8 15.3 collective-permute-start.3
  412.4 105.4 %copy-start.12 = (f32[2,256,256]{2,1,0:T(8,128)}, f32[2,256,256]{2,1,0:T(8,128)S(1)}, u32[]{:S(2)}) copy-start(f32[2,256,256]{2,1,0:T(8,128)S(1)} %fusion.84) | copy-start | bytes 1572868
  412.4 11.6 collective-permute-start.4
  424.2 92.1 %collective-permute-start.5 = (f32[2,256,512]{2,1,0:T(8,128)S(1)}, f32[2,256,512]{2,1,0:T(8,128)}, u32[]{:S(2)}, u32[]{:S(2)}) collective-permute-start(f32[2,256,512]{2,1,0:T(8,128)S(1)} %pad_maximum_fusion.4), channel_id=1, source_target_pairs={{16,0},{32,16},{48,32},{64,48},{80,64},{96,80},{112,96},{17,1},{33... | collective-permute-start | bytes 3145736 | tf_op jit(solution)/shard_map/ppermute | solution.py:17
  809.6 30.8 %copy-start.20 = (f32[2,256,256]{2,1,0:T(8,128)S(1)}, f32[2,256,256]{2,1,0:T(8,128)}, u32[]{:S(2)}) copy-start(f32[2,256,256]{2,1,0:T(8,128)} %param.25) | copy-start | bytes 1572868
  841.4 3.0 copy-start.15
  841.6 2.9 copy-start.16
  862.8 4.5 copy-start.10
  891.1 4.7 copy-start.8
  1048.4 54.6 %copy-start.6 = (f32[3,512,512]{2,1,0:T(8,128)S(1)}, f32[3,512,512]{2,1,0:T(8,128)}, u32[]{:S(2)}) copy-start(f32[3,512,512]{2,1,0:T(8,128)} %get-tuple-element.271) | copy-start | bytes 9437188
  1050.2 52.8 %collective-permute-start.6 = (f32[3,256,512]{2,1,0:T(8,128)S(1)}, f32[3,256,512]{2,1,0:T(8,128)S(1)}, u32[]{:S(2)}, u32[]{:S(2)}) collective-permute-start(f32[3,256,512]{2,1,0:T(8,128)S(1)} %slice.177), channel_id=1, source_target_pairs={{0,16},{16,32},{32,48},{48,64},{64,80},{80,96},{96,112},{1,17},{17... | collective-permute-start | bytes 4718600 | tf_op jit(solution)/shard_map/ppermute | solution.py:17
  1103.3 19.9 %copy-start.13 = (f32[2,256,256]{2,1,0:T(8,128)S(1)}, f32[2,256,256]{2,1,0:T(8,128)}, u32[]{:S(2)}) copy-start(f32[2,256,256]{2,1,0:T(8,128)} %copy-done.12) | copy-start | bytes 1572868
  1103.4 19.6 %collective-permute-start.7 = (f32[3,256,256]{2,1,0:T(8,128)S(1)}, f32[3,256,256]{2,1,0:T(8,128)S(1)}, u32[]{:S(2)}, u32[]{:S(2)}) collective-permute-start(f32[3,256,256]{2,1,0:T(8,128)S(1)} %slice.227), channel_id=1, source_target_pairs={{0,1},{1,2},{2,3},{3,4},{4,5},{5,6},{6,7},{7,8},{8,9},{9,10},{10,1... | collective-permute-start | bytes 2359304 | tf_op jit(solution)/shard_map/ppermute | solution.py:17
Sparse Core Ops, SparseCore 0:
  215.1 594.4 all-gather.4
  904.6 597.8 all-gather.6
